TPU v7x, 512 devices: a whole 4x8x8 slice. The times are simulated.
512 devices in a mesh: expert: 8 (over x, y_hi), dp: 64 (over z, y_lo, core).
Axes of the slice: x: 4, y: 8 (y_hi: 2, y_lo: 4; y = y_hi * 4 + y_lo), z: 8, core: 2. Of those that a mesh axis runs over, the one named last changes fastest.
Arguments:
- tokens: bfloat16 [64, 16, 2048], P('dp', 'expert'), may hold values from -6 to 6
- out_grad: bfloat16 [64, 16, 2048], P('dp', 'expert'), may hold values from -6 to 6
- expert_ids: int32 [64, 16, 2], P('dp'), may hold values from 0 to 7, as said below
- gate_scores: bfloat16 [64, 16, 2], P('dp'), may hold values from 0.25 to 1
- w_gate: bfloat16 [8, 2048, 8192], P('expert', None, 'dp'), may hold values from -0.125 to 0.125
- w_up: bfloat16 [8, 2048, 8192], P('expert', None, 'dp'), may hold values from -0.125 to 0.125
- w_down: bfloat16 [8, 8192, 2048], P('expert', 'dp'), may hold values from -0.0625 to 0.0625
Outputs:
- token_grad: bfloat16 [64, 16, 2048], P('dp', 'expert')
- grad_gate: bfloat16 [8, 2048, 8192], P('expert', None, 'dp')
- grad_up: bfloat16 [8, 2048, 8192], P('expert', None, 'dp')
- grad_down: bfloat16 [8, 8192, 2048], P('expert', 'dp')
Inputs may be any that keep to these rules, and one draw needn't show every extreme that they name: `expert_ids`: each token names two different experts; within a group no expert is named by more than 7 tokens, and in every group some expert is named by exactly 7 tokens.
All inputs are finite; a program needn't handle non-finite values.
Results may differ from a plain program's by a relative error of at most 0.0058.
Values may be sent and summed in bfloat16 or wider, within the bound.
A program may use at most 64 MiB of HBM per device.

v0:
```python
import jax
import jax.numpy as jnp
from jax import lax
from jax.sharding import PartitionSpec as P


def slot_table(expert_ids, experts):
    expert_range = jnp.arange(experts, dtype=jnp.int32)
    naming = jnp.sum((expert_ids[..., :, None] == expert_range).astype(jnp.int32), axis=-2)
    before = jnp.cumsum(naming, axis=-2) - naming
    return jnp.take_along_axis(before, expert_ids, axis=-1)


def local(tokens, out_grad, expert_ids, gate_scores, w_gate, w_up, w_down):
    tok_dev = tokens.shape[1]
    group_tok = expert_ids.shape[1]
    capacity = min(2 * tok_dev + 3, group_tok)
    experts = lax.axis_size("expert")
    my_expert = lax.axis_index("expert")
    group_ids = expert_ids[0]
    group_slots = slot_table(group_ids, experts)
    group_x, group_dy = (
        lax.all_gather(tokens, "expert", axis=1, tiled=True),
        lax.all_gather(out_grad, "expert", axis=1, tiled=True),
    )
    slot_range = jnp.arange(capacity, dtype=jnp.int32)
    matches = (group_ids[None, :, :] == my_expert) & (
        group_slots[None, :, :] == slot_range[:, None, None]
    )
    placing = jnp.sum(matches.astype(jnp.float32), axis=-1)
    weighting = jnp.sum(
        matches.astype(jnp.float32) * gate_scores[0].astype(jnp.float32)[None, :, :], axis=-1
    )
    x_picked = jnp.dot(
        placing.astype(jnp.bfloat16), group_x[0], preferred_element_type=jnp.float32
    ).astype(jnp.bfloat16)
    dy_picked = jnp.dot(
        weighting.astype(jnp.bfloat16), group_dy[0], preferred_element_type=jnp.float32
    ).astype(jnp.bfloat16)
    gate_slab = w_gate[0]
    up_slab = w_up[0]
    down_slab = w_down[0]
    input_rows = lax.all_gather(x_picked, "dp", axis=0, tiled=True)
    pre_gate = jnp.dot(input_rows, gate_slab, preferred_element_type=jnp.float32)
    pre_up = jnp.dot(input_rows, up_slab, preferred_element_type=jnp.float32)
    sigmoid_gate = jax.nn.sigmoid(pre_gate)
    activated = pre_gate * sigmoid_gate
    hidden = (activated * pre_up).astype(jnp.bfloat16)
    grad_rows = lax.all_gather(dy_picked, "dp", axis=0, tiled=True)
    grad_down = jnp.dot(hidden.T, grad_rows, preferred_element_type=jnp.float32).astype(
        jnp.bfloat16
    )
    grad_hidden = jnp.dot(grad_rows, down_slab.T, preferred_element_type=jnp.float32)
    gate_delta = (
        grad_hidden * pre_up * sigmoid_gate * (1.0 + pre_gate * (1.0 - sigmoid_gate))
    ).astype(jnp.bfloat16)
    up_delta = (grad_hidden * activated).astype(jnp.bfloat16)
    grad_gate = jnp.dot(input_rows.T, gate_delta, preferred_element_type=jnp.float32).astype(
        jnp.bfloat16
    )
    grad_up = jnp.dot(input_rows.T, up_delta, preferred_element_type=jnp.float32).astype(
        jnp.bfloat16
    )
    total = jnp.dot(gate_delta, gate_slab.T, preferred_element_type=jnp.float32)
    row_grad = lax.psum_scatter(
        total + jnp.dot(up_delta, up_slab.T, preferred_element_type=jnp.float32),
        "dp",
        scatter_dimension=0,
        tiled=True,
    )
    partial_tokens = jnp.dot(
        placing.T, row_grad, precision=lax.Precision.HIGHEST, preferred_element_type=jnp.float32
    )
    token_grad = lax.psum_scatter(partial_tokens, "expert", scatter_dimension=0, tiled=True)
    return (token_grad.astype(jnp.bfloat16)[None], grad_gate[None], grad_up[None], grad_down[None])


def solution(mesh):
    return jax.shard_map(
        local,
        mesh=mesh,
        in_specs=(
            P("dp", "expert", None),
            P("dp", "expert", None),
            P("dp", None, None),
            P("dp", None, None),
            P("expert", None, "dp"),
            P("expert", None, "dp"),
            P("expert", "dp", None),
        ),
        out_specs=(
            P("dp", "expert", None),
            P("expert", None, "dp"),
            P("expert", None, "dp"),
            P("expert", "dp", None),
        ),
        check_vma=False,
    )
```

profile of v0, /device:TPU:64, one launch (start us, length us, event | category | flops | bytes accessed | tf_op | source)
XLA Modules:
  0.0 564.1 jit_solution(10592391072857889739)
XLA Ops:
  11.2 44.1 %all_gather.14 = bf16[1,16,2048]{2,0,1:T(2,128)(2,1)S(1)} all-gather(bf16[1,2,2048]{2,0,1:T(2,128)(2,1)S(1)} %copy.75), channel_id=1, replica_groups=mesh['expert'=8,'dp'=64] {'expert'}, dimensions={1}, use_global_device_ids=true | all-gather | bytes 73728 | tf_op jit(solution)/shard_map/all_gather | solution.py:23
  56.3 44.0 %all_gather.12 = bf16[1,16,2048]{2,0,1:T(2,128)(2,1)S(1)} all-gather(bf16[1,2,2048]{2,0,1:T(2,128)(2,1)S(1)} %copy.74), channel_id=1, replica_groups=mesh['expert'=8,'dp'=64] {'expert'}, dimensions={1}, use_global_device_ids=true | all-gather | bytes 73728 | tf_op jit(solution)/shard_map/all_gather | solution.py:24
  101.1 1.3 dynamic-slice.6
  102.4 1.3 dynamic-slice.2
  104.9 71.9 %all-gather.7.cloned.1.call-done = bf16[64,7,2048]{2,1,0:T(8,128)(2,1)} async-done(((bf16[1,7,2048]{2,1,0:T(8,128)(2,1)}), bf16[64,7,2048]{2,1,0:T(8,128)(2,1)}) %all-gather.7.cloned.1.call-update) | async-done | bytes 1835024 | tf_op jit(solution)/shard_map/all_gather | solution.py:43
  176.8 2.6 reshape.57
  181.1 114.7 %all-gather.5.cloned.1.call-done = bf16[64,7,2048]{2,1,0:T(8,128)(2,1)} async-done(((bf16[1,7,2048]{2,1,0:T(8,128)(2,1)}), bf16[64,7,2048]{2,1,0:T(8,128)(2,1)}) %all-gather.5.cloned.1.call-update) | async-done | bytes 1835024 | tf_op jit(solution)/shard_map/all_gather | solution.py:49
  295.8 3.7 reshape.55
  299.6 2.9 fusion.3
  303.8 2.4 convolution_add_fusion
  306.3 143.5 %fusion = f32[8,2048]{1,0:T(8,128)S(1)} fusion(f32[448,2048]{1,0:T(8,128)} %convolution_add_fusion), kind=kCustom, calls=%all-reduce-scatter | all-reduce-scatter fusion | flops 1048577 | bytes 3737600
  449.8 2.1 collective-permute-start.6
  451.9 1.9 collective-permute-start.5
  453.8 17.8 %collective-permute-start.7 = (f32[7,2048]{1,0:T(8,128)S(1)}, f32[7,2048]{1,0:T(8,128)S(1)}, u32[]{:S(2)}, u32[]{:S(2)}) collective-permute-start(f32[7,2048]{1,0:T(8,128)S(1)} %slice.2), channel_id=1, source_target_pairs={{0,8},{1,9},{2,10},{3,11},{4,12},{5,13},{6,14},{7,15},{8,16},{9,17... | collective-permute-start | bytes 172040
  471.7 1.6 fusion.2
  473.3 5.9 %collective-permute-start.4 = (f32[8,2048]{1,0:T(8,128)S(1)}, f32[8,2048]{1,0:T(8,128)S(1)}, u32[]{:S(2)}, u32[]{:S(2)}) collective-permute-start(f32[8,2048]{1,0:T(8,128)S(1)} %fusion), channel_id=1, source_target_pairs={{0,5},{1,6},{2,7},{3,8},{4,9},{5,10},{6,11},{7,12},{8,13},{9,14},{... | collective-permute-start | bytes 196616
  479.2 8.7 %collective-permute-start.3 = (f32[8,2048]{1,0:T(8,128)S(1)}, f32[8,2048]{1,0:T(8,128)S(1)}, u32[]{:S(2)}, u32[]{:S(2)}) collective-permute-start(f32[8,2048]{1,0:T(8,128)S(1)} %fusion), channel_id=1, source_target_pairs={{0,4},{1,5},{2,6},{3,7},{4,8},{5,9},{6,10},{7,11},{8,12},{9,13},{1... | collective-permute-start | bytes 196616
  487.8 1.9 collective-permute-start.2
  489.8 3.4 collective-permute-start.1
  493.2 2.3 collective-permute-start
  495.5 1.6 fusion.1
  497.1 1.7 collective-permute-done.1
  498.8 2.7 collective-permute-done
  502.9 53.8 %all-reduce.4 = bf16[16,2048]{1,0:T(8,128)(2,1)S(1)} all-reduce(f32[16,2048]{1,0:T(8,128)S(1)} %fusion.16), channel_id=3, replica_groups=mesh['expert'=8,'dp'=64] {'expert'}, use_global_device_ids=true, to_apply=%region_5.6.clone | all-reduce | flops 32768 | bytes 196608
  (54 shorter events, 10.7 us)
Async XLA Ops:
  7.2 172.3 %copy-start = (bf16[1,2048,128]{2,1,0:T(8,128)(2,1)S(1)}, bf16[1,2048,128]{2,1,0:T(8,128)(2,1)}, u32[]{:S(2)}) copy-start(bf16[1,2048,128]{2,1,0:T(8,128)(2,1)} %param.11) | copy-start | bytes 1572868
  7.2 169.6 %all-gather.7.cloned.1.call-start = ((), (), s32[]{:S(2)}) async-start(), calls=%async_computation.1 | async-start | bytes 2129920 | tf_op jit(solution)/shard_map/all_gather | solution.py:43
  10.3 0.9 copy-start.5
  10.3 0.9 copy-start.6
  10.3 46.0 %copy-start.7 = (bf16[1,2,2048]{2,1,0:T(2,128)(2,1)S(1)}, bf16[1,2,2048]{2,1,0:T(2,128)(2,1)}, u32[]{:S(2)}) copy-start(bf16[1,2,2048]{2,1,0:T(2,128)(2,1)} %param.8) | copy-start | bytes 24580
  56.2 239.6 %all-gather.5.cloned.1.call-start = ((), (), s32[]{:S(2)}) async-start(), calls=%async_computation | async-start | bytes 2129920 | tf_op jit(solution)/shard_map/all_gather | solution.py:49
  179.4 1.0 copy-start.2
  299.6 3.0 copy-start.1
  299.6 3.0 copy-start.8
  303.2 0.7 copy-start.3
  449.8 45.7 %copy-start.4 = (bf16[448,128]{1,0:T(8,128)(2,1)S(1)}, bf16[448,128]{1,0:T(8,128)(2,1)}, u32[]{:S(2)}) copy-start(bf16[448,128]{1,0:T(8,128)(2,1)} %copy-done.3) | copy-start | bytes 344068
  449.8 39.9 %collective-permute-start.6 = (f32[8,2048]{1,0:T(8,128)S(1)}, f32[8,2048]{1,0:T(8,128)S(1)}, u32[]{:S(2)}, u32[]{:S(2)}) collective-permute-start(f32[8,2048]{1,0:T(8,128)S(1)} %fusion), channel_id=1, source_target_pairs={{0,7},{1,8},{2,9},{3,10},{4,11},{5,12},{6,13},{7,14},{8,15},{9,16}... | collective-permute-start | bytes 196616
  451.9 41.2 %collective-permute-start.5 = (f32[8,2048]{1,0:T(8,128)S(1)}, f32[8,2048]{1,0:T(8,128)S(1)}, u32[]{:S(2)}, u32[]{:S(2)}) collective-permute-start(f32[8,2048]{1,0:T(8,128)S(1)} %fusion), channel_id=1, source_target_pairs={{0,6},{1,7},{2,8},{3,9},{4,10},{5,11},{6,12},{7,13},{8,14},{9,15},... | collective-permute-start | bytes 196616
  453.8 34.0 %collective-permute-start.7 = (f32[7,2048]{1,0:T(8,128)S(1)}, f32[7,2048]{1,0:T(8,128)S(1)}, u32[]{:S(2)}, u32[]{:S(2)}) collective-permute-start(f32[7,2048]{1,0:T(8,128)S(1)} %slice.2), channel_id=1, source_target_pairs={{0,8},{1,9},{2,10},{3,11},{4,12},{5,13},{6,14},{7,15},{8,16},{9,17... | collective-permute-start | bytes 172040
  473.3 23.8 %collective-permute-start.4 = (f32[8,2048]{1,0:T(8,128)S(1)}, f32[8,2048]{1,0:T(8,128)S(1)}, u32[]{:S(2)}, u32[]{:S(2)}) collective-permute-start(f32[8,2048]{1,0:T(8,128)S(1)} %fusion), channel_id=1, source_target_pairs={{0,5},{1,6},{2,7},{3,8},{4,9},{5,10},{6,11},{7,12},{8,13},{9,14},{... | collective-permute-start | bytes 196616
  479.2 17.9 %collective-permute-start.3 = (f32[8,2048]{1,0:T(8,128)S(1)}, f32[8,2048]{1,0:T(8,128)S(1)}, u32[]{:S(2)}, u32[]{:S(2)}) collective-permute-start(f32[8,2048]{1,0:T(8,128)S(1)} %fusion), channel_id=1, source_target_pairs={{0,4},{1,5},{2,6},{3,7},{4,8},{5,9},{6,10},{7,11},{8,12},{9,13},{1... | collective-permute-start | bytes 196616
  487.8 9.3 %collective-permute-start.2 = (f32[8,2048]{1,0:T(8,128)S(1)}, f32[8,2048]{1,0:T(8,128)S(1)}, u32[]{:S(2)}, u32[]{:S(2)}) collective-permute-start(f32[8,2048]{1,0:T(8,128)S(1)} %fusion), channel_id=1, source_target_pairs={{0,3},{1,4},{2,5},{3,6},{4,7},{5,8},{6,9},{7,10},{8,11},{9,12},{10... | collective-permute-start | bytes 196616
  489.8 9.0 %collective-permute-start.1 = (f32[8,2048]{1,0:T(8,128)S(1)}, f32[8,2048]{1,0:T(8,128)S(1)}, u32[]{:S(2)}, u32[]{:S(2)}) collective-permute-start(f32[8,2048]{1,0:T(8,128)S(1)} %fusion), channel_id=1, source_target_pairs={{0,2},{1,3},{2,4},{3,5},{4,6},{5,7},{6,8},{7,9},{8,10},{9,11},{10,... | collective-permute-start | bytes 196616
  493.2 8.3 %collective-permute-start = (f32[8,2048]{1,0:T(8,128)S(1)}, f32[8,2048]{1,0:T(8,128)S(1)}, u32[]{:S(2)}, u32[]{:S(2)}) collective-permute-start(f32[8,2048]{1,0:T(8,128)S(1)} %fusion), channel_id=1, source_target_pairs={{0,1},{1,2},{2,3},{3,4},{4,5},{5,6},{6,7},{7,8},{8,9},{9,10},{10,1... | collective-permute-start | bytes 196616
Sparse Core Ops, SparseCore 0:
  56.3 120.4 all-gather.6
  179.5 116.2 all-gather.4
where the time goes:
time: 565 us; the launch traced here: 564 us
  blocking collectives  285 us (50%)
  waiting for transfers between devices  191 us (34%)
  starting transfers between devices  44 us (8%)
  between operations  15.6 us (3%)
  matrix products  13 us (2%)
  local copies, waits for them, and re-layouts  12.1 us (2%)
    unnamed x2, blocking collectives  197 us
    all_gather x1, waiting for transfers between devices, local(): grad_rows = lax.all_gather(dy_picked, 'dp', axis=0, tiled=True)  115 us
    all_gather x1, waiting for transfers between devices, local(): input_rows = lax.all_gather(x_picked, 'dp', axis=0, tiled=True)  71.9 us
    all_gather x1, blocking collectives, local(): lax.all_gather(tokens, 'expert', axis=1, tiled=True)  44.1 us
    all_gather x1, blocking collectives, local(): lax.all_gather(out_grad, 'expert', axis=1, tiled=True)  44 us
    unnamed x8, starting transfers between devices  43.9 us
  transfers between devices with their start and end apart: 10, of which 4 were waited for; matrix products, arithmetic and copies ran while one was open for 2% of the time, Pallas kernels for 0%

commit v1 on v0

--- a/solution.py
+++ b/solution.py
@@ -40,7 +40,15 @@
     gate_slab = w_gate[0]
     up_slab = w_up[0]
     down_slab = w_down[0]
-    input_rows = lax.all_gather(x_picked, "dp", axis=0, tiled=True)
+    input_rows = jnp.concatenate(
+        lax.all_to_all(
+            jnp.stack(tuple((x_picked for _ in range(lax.axis_size("dp"))))),
+            axis_name="dp",
+            split_axis=0,
+            concat_axis=0,
+        ),
+        axis=0,
+    )
     pre_gate = jnp.dot(input_rows, gate_slab, preferred_element_type=jnp.float32)
     pre_up = jnp.dot(input_rows, up_slab, preferred_element_type=jnp.float32)
     sigmoid_gate = jax.nn.sigmoid(pre_gate)

time: 565 us -> 530 us (0.938)
  waiting for transfers between devices: 191 us -> 110 us
  blocking collectives: 285 us -> 316 us
  starting transfers between devices: 44 us -> 57.7 us
    all_gather x1 -> x0, waiting for transfers between devices: 71.9 us -> none  [local(): input_rows = lax.all_gather(x_picked, 'dp', axis=0, tiled=True)]
    all_gather x1, blocking collectives: 44 us -> 75 us  [local(): lax.all_gather(out_grad, 'expert', axis=1, tiled=True)]
    all_to_all x0 -> x1, starting transfers between devices: none -> 13.8 us  [local(): lax.all_to_all(jnp.stack(tuple((x_picked for _ in range(lax.axis_size('dp...]
    all_gather x1, waiting for transfers between devices: 115 us -> 105 us  [local(): grad_rows = lax.all_gather(dy_picked, 'dp', axis=0, tiled=True)]
  transfers between devices with their start and end apart: 10 -> 10, of which waited for: 4 -> 3; matrix products, arithmetic and copies ran while one was open for 2% -> 2% of each run, Pallas kernels for 0% -> 0%
where the time goes in v1:
time: 530 us; the launch traced here: 529 us
  blocking collectives  316 us (60%)
  waiting for transfers between devices  110 us (21%)
  starting transfers between devices  57.7 us (11%)
  between operations  15.6 us (3%)
  local copies, waits for them, and re-layouts  13.7 us (3%)
  matrix products  12.4 us (2%)
    unnamed x2, blocking collectives  197 us
    all_gather x1, waiting for transfers between devices, local(): grad_rows = lax.all_gather(dy_picked, 'dp', axis=0, tiled=True)  105 us
    all_gather x1, blocking collectives, local(): lax.all_gather(out_grad, 'expert', axis=1, tiled=True)  75 us
    all_gather x1, blocking collectives, local(): lax.all_gather(tokens, 'expert', axis=1, tiled=True)  44.1 us
    unnamed x8, starting transfers between devices  43.9 us
    all_to_all x1, starting transfers between devices, local(): lax.all_to_all(jnp.stack(tuple((x_picked for _ in range(lax.axis_size('dp...  13.8 us
  transfers between devices with their start and end apart: 10, of which 3 were waited for; matrix products, arithmetic and copies ran while one was open for 2% of the time, Pallas kernels for 0%

profile of v1, /device:TPU:64, one launch (start us, length us, event | category | flops | bytes accessed | tf_op | source)
XLA Modules:
  0.0 528.7 jit_solution(9808620005610312488)
XLA Ops:
  11.2 44.1 %all_gather.11 = bf16[1,16,2048]{2,0,1:T(2,128)(2,1)S(1)} all-gather(bf16[1,2,2048]{2,0,1:T(2,128)(2,1)S(1)} %copy.75), channel_id=1, replica_groups=mesh['expert'=8,'dp'=64] {'expert'}, dimensions={1}, use_global_device_ids=true | all-gather | bytes 73728 | tf_op jit(solution)/shard_map/all_gather | solution.py:23
  55.5 1.6 stack.2
  57.1 13.8 %all-to-all-start = ((bf16[64,7,2048]{2,1,0:T(8,128)(2,1)}), bf16[64,7,2048]{2,1,0:T(8,128)(2,1)}, u32[]{:S(2)}, u32[]{:S(2)}) async-start(bf16[64,7,2048]{2,1,0:T(8,128)(2,1)} %stack.2), calls=%async_computation | async-start | bytes 4194304 | tf_op jit(solution)/shard_map/all_to_all | solution.py:44
  71.0 75.0 %all_gather.9 = bf16[1,16,2048]{2,0,1:T(2,128)(2,1)S(1)} all-gather(bf16[1,2,2048]{2,0,1:T(2,128)(2,1)S(1)} %copy.74), channel_id=1, replica_groups=mesh['expert'=8,'dp'=64] {'expert'}, dimensions={1}, use_global_device_ids=true | all-gather | bytes 73728 | tf_op jit(solution)/shard_map/all_gather | solution.py:24
  146.8 1.3 dynamic-slice.6
  150.6 2.6 reshape.51
  154.9 105.5 %all-gather.3.cloned.1.call-done = bf16[64,7,2048]{2,1,0:T(8,128)(2,1)} async-done(((bf16[1,7,2048]{2,1,0:T(8,128)(2,1)}), bf16[64,7,2048]{2,1,0:T(8,128)(2,1)}) %all-gather.3.cloned.1.call-update) | async-done | bytes 1835024 | tf_op jit(solution)/shard_map/all_gather | solution.py:57
  260.4 3.7 reshape.61
  264.1 3.0 fusion.3
  268.4 2.4 convolution_add_fusion
  270.9 143.6 %fusion = f32[8,2048]{1,0:T(8,128)S(1)} fusion(f32[448,2048]{1,0:T(8,128)} %convolution_add_fusion), kind=kCustom, calls=%all-reduce-scatter | all-reduce-scatter fusion | flops 1048577 | bytes 3737600
  414.4 2.1 collective-permute-start.6
  416.5 1.9 collective-permute-start.5
  418.4 17.8 %collective-permute-start.7 = (f32[7,2048]{1,0:T(8,128)S(1)}, f32[7,2048]{1,0:T(8,128)S(1)}, u32[]{:S(2)}, u32[]{:S(2)}) collective-permute-start(f32[7,2048]{1,0:T(8,128)S(1)} %slice.2), channel_id=1, source_target_pairs={{0,8},{1,9},{2,10},{3,11},{4,12},{5,13},{6,14},{7,15},{8,16},{9,17... | collective-permute-start | bytes 172040
  436.3 1.6 fusion.2
  437.9 5.9 %collective-permute-start.4 = (f32[8,2048]{1,0:T(8,128)S(1)}, f32[8,2048]{1,0:T(8,128)S(1)}, u32[]{:S(2)}, u32[]{:S(2)}) collective-permute-start(f32[8,2048]{1,0:T(8,128)S(1)} %fusion), channel_id=1, source_target_pairs={{0,5},{1,6},{2,7},{3,8},{4,9},{5,10},{6,11},{7,12},{8,13},{9,14},{... | collective-permute-start | bytes 196616
  443.8 8.7 %collective-permute-start.3 = (f32[8,2048]{1,0:T(8,128)S(1)}, f32[8,2048]{1,0:T(8,128)S(1)}, u32[]{:S(2)}, u32[]{:S(2)}) collective-permute-start(f32[8,2048]{1,0:T(8,128)S(1)} %fusion), channel_id=1, source_target_pairs={{0,4},{1,5},{2,6},{3,7},{4,8},{5,9},{6,10},{7,11},{8,12},{9,13},{1... | collective-permute-start | bytes 196616
  452.4 1.9 collective-permute-start.2
  454.4 3.4 collective-permute-start.1
  457.8 2.3 collective-permute-start
  460.1 1.6 fusion.1
  461.7 1.7 collective-permute-done.1
  463.4 2.7 collective-permute-done
  467.5 53.8 %all-reduce.4 = bf16[16,2048]{1,0:T(8,128)(2,1)S(1)} all-reduce(f32[16,2048]{1,0:T(8,128)S(1)} %fusion.15), channel_id=3, replica_groups=mesh['expert'=8,'dp'=64] {'expert'}, use_global_device_ids=true, to_apply=%region_5.6.clone | all-reduce | flops 32768 | bytes 196608
  (54 shorter events, 11.3 us)
Async XLA Ops:
  7.2 146.0 %copy-start = (bf16[1,2048,128]{2,1,0:T(8,128)(2,1)S(1)}, bf16[1,2048,128]{2,1,0:T(8,128)(2,1)}, u32[]{:S(2)}) copy-start(bf16[1,2048,128]{2,1,0:T(8,128)(2,1)} %param.11) | copy-start | bytes 1572868
  10.2 0.9 copy-start.5
  10.3 0.9 copy-start.6
  57.1 13.8 %copy-start.7 = (bf16[1,2,2048]{2,1,0:T(2,128)(2,1)S(1)}, bf16[1,2,2048]{2,1,0:T(2,128)(2,1)}, u32[]{:S(2)}) copy-start(bf16[1,2,2048]{2,1,0:T(2,128)(2,1)} %param.8) | copy-start | bytes 24580
  57.1 93.5 %all-to-all-start = ((bf16[64,7,2048]{2,1,0:T(8,128)(2,1)}), bf16[64,7,2048]{2,1,0:T(8,128)(2,1)}, u32[]{:S(2)}, u32[]{:S(2)}) async-start(bf16[64,7,2048]{2,1,0:T(8,128)(2,1)} %stack.2), calls=%async_computation | async-start | bytes 4194304 | tf_op jit(solution)/shard_map/all_to_all | solution.py:44
  70.9 189.5 %all-gather.3.cloned.1.call-start = ((), (), s32[]{:S(2)}) async-start(), calls=%async_computation.1 | async-start | bytes 2129920 | tf_op jit(solution)/shard_map/all_gather | solution.py:57
  153.2 1.0 copy-start.2
  264.1 3.0 copy-start.1
  264.1 3.0 copy-start.8
  267.7 0.7 copy-start.3
  414.4 45.7 %copy-start.4 = (bf16[448,128]{1,0:T(8,128)(2,1)S(1)}, bf16[448,128]{1,0:T(8,128)(2,1)}, u32[]{:S(2)}) copy-start(bf16[448,128]{1,0:T(8,128)(2,1)} %copy-done.3) | copy-start | bytes 344068
  414.4 39.9 %collective-permute-start.6 = (f32[8,2048]{1,0:T(8,128)S(1)}, f32[8,2048]{1,0:T(8,128)S(1)}, u32[]{:S(2)}, u32[]{:S(2)}) collective-permute-start(f32[8,2048]{1,0:T(8,128)S(1)} %fusion), channel_id=1, source_target_pairs={{0,7},{1,8},{2,9},{3,10},{4,11},{5,12},{6,13},{7,14},{8,15},{9,16}... | collective-permute-start | bytes 196616
  416.5 41.3 %collective-permute-start.5 = (f32[8,2048]{1,0:T(8,128)S(1)}, f32[8,2048]{1,0:T(8,128)S(1)}, u32[]{:S(2)}, u32[]{:S(2)}) collective-permute-start(f32[8,2048]{1,0:T(8,128)S(1)} %fusion), channel_id=1, source_target_pairs={{0,6},{1,7},{2,8},{3,9},{4,10},{5,11},{6,12},{7,13},{8,14},{9,15},... | collective-permute-start | bytes 196616
  418.4 34.0 %collective-permute-start.7 = (f32[7,2048]{1,0:T(8,128)S(1)}, f32[7,2048]{1,0:T(8,128)S(1)}, u32[]{:S(2)}, u32[]{:S(2)}) collective-permute-start(f32[7,2048]{1,0:T(8,128)S(1)} %slice.2), channel_id=1, source_target_pairs={{0,8},{1,9},{2,10},{3,11},{4,12},{5,13},{6,14},{7,15},{8,16},{9,17... | collective-permute-start | bytes 172040
  437.9 23.8 %collective-permute-start.4 = (f32[8,2048]{1,0:T(8,128)S(1)}, f32[8,2048]{1,0:T(8,128)S(1)}, u32[]{:S(2)}, u32[]{:S(2)}) collective-permute-start(f32[8,2048]{1,0:T(8,128)S(1)} %fusion), channel_id=1, source_target_pairs={{0,5},{1,6},{2,7},{3,8},{4,9},{5,10},{6,11},{7,12},{8,13},{9,14},{... | collective-permute-start | bytes 196616
  443.8 17.9 %collective-permute-start.3 = (f32[8,2048]{1,0:T(8,128)S(1)}, f32[8,2048]{1,0:T(8,128)S(1)}, u32[]{:S(2)}, u32[]{:S(2)}) collective-permute-start(f32[8,2048]{1,0:T(8,128)S(1)} %fusion), channel_id=1, source_target_pairs={{0,4},{1,5},{2,6},{3,7},{4,8},{5,9},{6,10},{7,11},{8,12},{9,13},{1... | collective-permute-start | bytes 196616
  452.4 9.3 %collective-permute-start.2 = (f32[8,2048]{1,0:T(8,128)S(1)}, f32[8,2048]{1,0:T(8,128)S(1)}, u32[]{:S(2)}, u32[]{:S(2)}) collective-permute-start(f32[8,2048]{1,0:T(8,128)S(1)} %fusion), channel_id=1, source_target_pairs={{0,3},{1,4},{2,5},{3,6},{4,7},{5,8},{6,9},{7,10},{8,11},{9,12},{10... | collective-permute-start | bytes 196616
  454.4 9.0 %collective-permute-start.1 = (f32[8,2048]{1,0:T(8,128)S(1)}, f32[8,2048]{1,0:T(8,128)S(1)}, u32[]{:S(2)}, u32[]{:S(2)}) collective-permute-start(f32[8,2048]{1,0:T(8,128)S(1)} %fusion), channel_id=1, source_target_pairs={{0,2},{1,3},{2,4},{3,5},{4,6},{5,7},{6,8},{7,9},{8,10},{9,11},{10,... | collective-permute-start | bytes 196616
  457.8 8.3 %collective-permute-start = (f32[8,2048]{1,0:T(8,128)S(1)}, f32[8,2048]{1,0:T(8,128)S(1)}, u32[]{:S(2)}, u32[]{:S(2)}) collective-permute-start(f32[8,2048]{1,0:T(8,128)S(1)} %fusion), channel_id=1, source_target_pairs={{0,1},{1,2},{2,3},{3,4},{4,5},{5,6},{6,7},{7,8},{8,9},{9,10},{10,1... | collective-permute-start | bytes 196616
Sparse Core Ops, SparseCore 0:
  146.9 113.4 all-gather.2
